TPU v7x, 32 devices: a whole 2x2x4 slice. The times are simulated.
32 devices in a mesh: groups: 2 (over x), dtp: 16 (over z, y, core).
Axes of the slice: x: 2, y: 2, z: 4, core: 2. Of those that a mesh axis runs over, the one named last changes fastest.
Arguments:
- grad_dec: bfloat16 [64, 8192], P(('groups', 'dtp')), parts along dimension 0, may hold values from -6 to 6
- token_order: int32 [64], P('groups'), parts along dimension 0, may hold values from 0 to 31, each once
- proj_pre_codes: bfloat16 [64, 8192], P('groups', 'dtp'), parts along dimension 0, may hold values from -4 to 4
- proj_pre_exps: int32 [64, 64], P('groups', 'dtp'), parts along dimension 0, may hold values from 6 to 10
- projector_norm_input_codes: bfloat16 [64, 12800], P(('groups', 'dtp')), parts along dimension 0, may hold values from -4 to 4
- projector_norm_input_exponents: int32 [64, 100], P(('groups', 'dtp')), parts along dimension 0, may hold values from 6 to 10
- projector_norm_gain: float32 [12800], replicated, may hold values from 0.1 to 1.9
- projector_norm_bias: float32 [12800], replicated, may hold values from -3 to 3
- proj_weight: bfloat16 [12800, 8192], P(None, 'dtp'), may hold values from -0.0546875 to 0.0546875
- vit_pre_codes: bfloat16 [256, 12800], P('groups', 'dtp'), parts along dimension 0, may hold values from -4 to 4
- vit_pre_exps: int32 [2, 12800], P('groups', 'dtp'), parts along dimension 0, may hold values from 6 to 10
- vit_down: bfloat16 [12800, 3200], P('dtp'), may hold values from -0.0546875 to 0.0546875
- vit_up: bfloat16 [3200, 12800], P(None, 'dtp'), may hold values from -0.109375 to 0.109375
- vit_mid_codes: bfloat16 [256, 3200], P(('groups', 'dtp')), parts along dimension 0, may hold values from -4 to 4
- vit_mid_exps: int32 [256, 25], P(('groups', 'dtp')), parts along dimension 0, may hold values from 6 to 10
- mid_gain: float32 [3200], replicated, may hold values from 0.1 to 1.9
- layer_scale: float32 [3200], replicated, may hold values from 0.25 to 1
Outputs:
- grad_proj_weight: bfloat16 [12800, 16384], P(None, ('groups', 'dtp')), parts along dimension 1
- grad_vit_down: bfloat16 [12800, 6400], P('dtp', 'groups'), parts along dimension 1
- grad_vit_up: bfloat16 [3200, 25600], P(None, ('groups', 'dtp')), parts along dimension 1
- grad_vit_in: bfloat16 [256, 3200], P(('groups', 'dtp')), parts along dimension 0
There are 2 independent parts, one for each index of `groups`. A program takes and returns all parts, laid end to end along the dimension named above; an argument that names none is the same for every part. Nothing has to cross between parts.
Inputs may be any that keep to these rules, and one draw needn't show every extreme that they name: A permutation: decoder position p holds encoder token token_order[p].
All inputs are finite; a program needn't handle non-finite values.
Results may differ from a plain program's by a relative error of at most 0.0075.
Values may be sent and summed in bfloat16 or wider, within the bound.
A program may use at most 128 MiB of HBM per device.

v0:
```python
import math

import jax
import jax.numpy as jnp
from jax import lax
from jax.sharding import PartitionSpec as P


def decode_block_columns(codes, exps):
    rows, cols = codes.shape
    groups = exps.shape[1]
    scale = jnp.exp2((exps - 8).astype(jnp.float32))
    return (
        codes.astype(jnp.float32).reshape(rows, groups, cols // groups) * scale[:, :, None]
    ).reshape(rows, cols)


def dequant_rows(codes, exps):
    rows, cols = codes.shape
    groups = exps.shape[0]
    scale = jnp.exp2((exps - 8).astype(jnp.float32))
    return (
        codes.astype(jnp.float32).reshape(groups, rows // groups, cols) * scale[:, None, :]
    ).reshape(rows, cols)


def gelu_grad(value):
    return 0.5 * (1.0 + jax.scipy.special.erf(value / math.sqrt(2.0))) + value * jnp.exp(
        -0.5 * value * value
    ) / math.sqrt(2.0 * math.pi)


def layer_norm_statistics(merged):
    center = merged - jnp.mean(merged, axis=-1, keepdims=True)
    inverse_deviation = lax.rsqrt(jnp.mean(center * center, axis=-1, keepdims=True) + 1e-05)
    return (center * inverse_deviation, inverse_deviation)


def layer_norm_backward(gradient_input, centered_unit_input, inverse_deviation, norm_gain_vector):
    gain_scaled_gradient = gradient_input * norm_gain_vector
    leading_moment = jnp.mean(gain_scaled_gradient, axis=-1, keepdims=True)
    trailing_moment = jnp.mean(gain_scaled_gradient * centered_unit_input, axis=-1, keepdims=True)
    return inverse_deviation * (
        gain_scaled_gradient - leading_moment - centered_unit_input * trailing_moment
    )


def rms_stats(mid):
    recip = lax.rsqrt(jnp.mean(mid * mid, axis=-1, keepdims=True) + 1e-06)
    return (mid * recip, recip)


def rms_back(gradient_input, uhat, recip, norm_gain_vector):
    gain_scaled_gradient = gradient_input * norm_gain_vector
    return recip * (
        gain_scaled_gradient - uhat * jnp.mean(gain_scaled_gradient * uhat, axis=-1, keepdims=True)
    )


def contract_rows(left, right):
    return lax.dot_general(
        left, right, (((0,), (0,)), ((), ())), preferred_element_type=jnp.float32
    )


def contract_cols(left, right):
    return lax.dot_general(
        left, right, (((1,), (1,)), ((), ())), preferred_element_type=jnp.float32
    )


def body(
    grad_dec,
    token_order,
    proj_pre_codes,
    proj_pre_exps,
    projector_norm_input_codes,
    projector_norm_input_exponents,
    projector_norm_gain,
    projector_norm_bias,
    proj_weight,
    vit_pre_codes,
    vit_pre_exps,
    vit_down,
    vit_up,
    vit_mid_codes,
    vit_mid_exps,
    mid_gain,
    layer_scale,
):
    f32 = jnp.float32
    brain_float_half = jnp.bfloat16
    own_vit = vit_mid_codes.shape[0]
    d_vit = vit_mid_codes.shape[1]
    uhat, recip = rms_stats(decode_block_columns(vit_mid_codes, vit_mid_exps))
    mid_normed = (uhat * mid_gain).astype(brain_float_half)
    received = lax.all_to_all(grad_dec, "dtp", split_axis=1, concat_axis=0, tiled=True)
    inverse = jnp.argsort(token_order)
    grad_act = jnp.take(received, inverse, axis=0)
    proj_pre = decode_block_columns(proj_pre_codes, proj_pre_exps)
    grad_pre = (grad_act.astype(f32) * gelu_grad(proj_pre)).astype(brain_float_half)
    pre = dequant_rows(vit_pre_codes, vit_pre_exps)
    hidden = jax.nn.gelu(pre, approximate=False).astype(brain_float_half)
    vit_rows_all = hidden.shape[0]
    merged_token_codes, merged_token_exponents = (
        lax.all_gather(projector_norm_input_codes, "dtp", axis=0, tiled=True),
        lax.all_gather(projector_norm_input_exponents, "dtp", axis=0, tiled=True),
    )
    centered_unit_input, inverse_deviation = layer_norm_statistics(
        decode_block_columns(merged_token_codes, merged_token_exponents)
    )
    normalized_rows = (centered_unit_input * projector_norm_gain + projector_norm_bias).astype(
        brain_float_half
    )
    grad_proj_weight = contract_rows(normalized_rows, grad_pre).astype(brain_float_half)
    normalized_gradient = contract_cols(grad_pre, proj_weight)
    merged_gradient_term = layer_norm_backward(
        normalized_gradient, centered_unit_input, inverse_deviation, projector_norm_gain
    )
    merged_token_gradient = lax.psum(merged_gradient_term, "dtp").astype(brain_float_half)
    grad_out_all = merged_token_gradient.reshape(vit_rows_all, d_vit)
    grad_out = lax.dynamic_slice_in_dim(grad_out_all, lax.axis_index("dtp") * own_vit, own_vit, 0)
    branch = (grad_out_all.astype(f32) * layer_scale).astype(brain_float_half)
    down_total = contract_rows(hidden, branch)
    grad_hidden = contract_cols(branch, vit_down)
    down_total, grad_hidden = (down_total, grad_hidden)
    grad_vit_down = down_total.astype(brain_float_half)
    grad_vit_pre = (grad_hidden * gelu_grad(pre)).astype(brain_float_half)
    rows = grad_vit_pre
    grad_vit_up = contract_rows(lax.all_gather(mid_normed, "dtp", axis=0, tiled=True), rows).astype(
        brain_float_half
    )
    rows = grad_vit_pre
    grad_mid_normed = lax.psum_scatter(
        contract_cols(rows, vit_up), "dtp", scatter_dimension=0, tiled=True
    )
    grad_vit_in = (grad_out.astype(f32) + rms_back(grad_mid_normed, uhat, recip, mid_gain)).astype(
        brain_float_half
    )
    return (grad_proj_weight, grad_vit_down, grad_vit_up, grad_vit_in)


def solution(mesh):
    return jax.shard_map(
        body,
        mesh=mesh,
        in_specs=(
            P(("groups", "dtp"), None),
            P("groups"),
            P("groups", "dtp"),
            P("groups", "dtp"),
            P(("groups", "dtp"), None),
            P(("groups", "dtp"), None),
            P(),
            P(),
            P(None, "dtp"),
            P("groups", "dtp"),
            P("groups", "dtp"),
            P("dtp", None),
            P(None, "dtp"),
            P(("groups", "dtp"), None),
            P(("groups", "dtp"), None),
            P(),
            P(),
        ),
        out_specs=(
            P(None, ("groups", "dtp")),
            P("dtp", "groups"),
            P(None, ("groups", "dtp")),
            P(("groups", "dtp"), None),
        ),
        check_vma=False,
    )
```

profile of v0, /device:TPU:0, one launch (start us, length us, event | category | flops | bytes accessed | tf_op | source)
XLA Modules:
  0.0 292.0 jit_solution(2263496778461031563)
XLA Ops:
  7.2 7.4 %all-to-all-start = ((bf16[2,16,512]{2,0,1:T(2,128)(2,1)}), bf16[2,16,512]{2,0,1:T(2,128)(2,1)S(1)}, u32[]{:S(2)}, u32[]{:S(2)}) async-start(bf16[2,16,512]{2,0,1:T(2,128)(2,1)} %bitcast.46), calls=%async_computation | async-start | bytes 65536 | tf_op jit(solution)/shard_map/all_to_all | solution.py:97
  14.6 0.0 all-reduce.4.cloned.1.call-start
  14.6 2.3 sort.17
  16.9 0.0 copy-start.24
  16.9 24.3 %all-gather = bf16[16,2,12800]{2,1,0:T(2,128)(2,1)S(1)} all-gather(bf16[1,2,12800]{2,1,0:T(2,128)(2,1)} %bitcast.45), channel_id=1, replica_groups=mesh['groups'=2,'dtp'=16] {'dtp'}, dimensions={0}, use_global_device_ids=true | all-gather | bytes 870400 | tf_op jit(solution)/shard_map/all_gather | solution.py:106
  41.3 0.2 reshape.158
  41.5 17.5 %all-gather.1 = s32[16,2,100]{2,1,0:T(2,128)S(1)} all-gather(s32[1,2,100]{2,1,0:T(2,128)S(1)} %bitcast.47), channel_id=1, replica_groups=mesh['groups'=2,'dtp'=16] {'dtp'}, dimensions={0}, use_global_device_ids=true | all-gather | bytes 13600 | tf_op jit(solution)/shard_map/all_gather | solution.py:107
  59.0 0.5 mul.205
  59.5 0.5 fusion.95
  60.0 0.0 copy-start.11
  60.0 0.0 copy-start.21
  60.0 0.0 copy-start.19
  60.0 0.0 copy-start.1
  60.0 0.0 copy-start.26
  60.0 0.0 copy-start.2
  60.0 0.0 copy-start.8
  60.1 0.4 multiply_reduce_fusion.1
  60.5 0.2 copy-done.23
  60.7 0.1 copy.28
  60.8 0.6 exponential_reduce_fusion
  61.4 0.1 copy.29
  61.5 0.2 multiply_reduce_fusion.3
  61.7 0.5 add_rsqrt_fusion
  62.3 0.6 dynamic-slice
  63.6 0.6 gather_fusion
  64.2 0.0 copy-start.3
  64.2 0.1 mul.213
  64.3 8.8 %fusion.94 = (f32[32]{0:T(128)S(1)}, f32[32]{0:T(128)S(1)}, f32[32,12800]{1,0:T(8,128)S(1)}) fusion(f32[32]{0:T(128)S(1)} %add_rsqrt_fusion.1, f32[32,12800]{1,0:T(8,128)S(1)} %get-tuple-element.9, f32[32]{0:T(128)S(1)} %broadcast_multiply_fusion.3, f32[12800]{0:T(1024)S(1)} %copy-done.2, bf16[12800,512]{1,0:T(8,128)(2,1)} %param.25, ...), kind=kOutput, calls=%fused_computation.136 | convolution fusion | flops 422117312 | bytes 16566816 | tf_op jit(solution)/shard_map/dot_general | solution.py:67
  73.1 1.6 subtract_multiply_fusion
  74.7 72.9 %all-reduce.5 = bf16[32,12800]{1,0:T(8,128)(2,1)S(1)} all-reduce(f32[32,12800]{1,0:T(8,128)} %subtract_multiply_fusion), channel_id=1, replica_groups=mesh['groups'=2,'dtp'=16] {'dtp'}, use_global_device_ids=true, to_apply=%region_5.6 | all-reduce | flops 409600 | bytes 2457600 | tf_op jit(solution)/shard_map/psum | solution.py:120
  147.6 1.6 reshape.144
  149.1 0.1 multiply_convert_fusion.1
  149.3 0.0 slice-start
  149.3 1.6 convert_element_type.90
  150.9 0.0 slice-start.1
  150.9 6.1 %convolution_convert_fusion.2 = bf16[800,3200]{1,0:T(8,128)(2,1)} fusion(bf16[128,3200]{1,0:T(8,128)(2,1)} %convert_element_type.90, bf16[128,800]{0,1:T(8,128)(2,1)} %param.26, f32[800]{0:T(1024)} %exponential_reduce_fusion), kind=kOutput, calls=%fused_computation.4 | convolution fusion | flops 664780800 | bytes 6147200 | tf_op jit(solution)/shard_map/dot_general | solution.py:61
  157.0 4.0 %fusion = bf16[128,800]{0,1:T(8,128)(2,1)S(1)} fusion(bf16[800,3200]{1,0:T(8,128)(2,1)} %param.28, bf16[128,3200]{1,0:T(8,128)(2,1)S(1)} %copy-done, f32[3200]{0:T(1024)S(1)} %copy-done.12, bf16[128,800]{0,1:T(8,128)(2,1)S(1)} %copy-done.25, f32[800]{0:T(1024)S(1)} %copy-done.20), kind=kOutput, calls=%fused_computation.14 | convolution fusion | flops 657817600 | bytes 6364800 | tf_op jit(solution)/shard_map/dot_general | solution.py:67
  161.0 2.2 fusion.96
  163.3 0.0 all-reduce.4.cloned.1.call-update
  163.3 0.7 copy-done.4
  164.0 0.1 copy-done.7
  164.1 0.0 copy-start.10
  164.2 7.0 %convolution_convert_fusion = bf16[12800,512]{1,0:T(8,128)(2,1)} fusion(f32[32,12800]{1,0:T(8,128)S(1)} %get-tuple-element.9, f32[12800]{0:T(1024)S(1)} %copy-done.7, f32[12800]{0:T(1024)S(1)} %copy-done.2, f32[32]{0:T(128)S(1)} %copy-done.16, f32[32]{0:T(128)S(1)} %copy-done.14, f32[4,8,4,128]{3,2,1,0:T(4,128)S(1)} %bitcast.42, ...), kind=kOutput, calls=%fused_computation.1 | convolution fusion | flops 428261376 | bytes 14979360 | tf_op jit(solution)/shard_map/dot_general | solution.py:61
  171.1 85.6 %all-reduce.4.cloned.1.call-done = f32[128,3200]{1,0:T(8,128)} async-done(((f32[128,3200]{1,0:T(8,128)}), f32[128,3200]{1,0:T(8,128)}) %all-reduce.4.cloned.1.call-update) | async-done | bytes 1638416
  256.7 1.1 multiply_reduce_fusion.2
  257.9 1.7 add_convert_fusion.2
  259.5 21.8 %all_gather.11 = bf16[128,3200]{1,0:T(8,128)(2,1)S(1)} all-gather(bf16[8,3200]{1,0:T(8,128)(2,1)S(1)} %get-tuple-element.11), channel_id=1, replica_groups=mesh['groups'=2,'dtp'=16] {'dtp'}, dimensions={0}, use_global_device_ids=true | all-gather | bytes 870400 | tf_op jit(solution)/shard_map/all_gather | solution.py:130
  281.3 3.8 %convolution_convert_fusion.1 = bf16[3200,800]{0,1:T(8,128)(2,1)} fusion(bf16[128,800]{0,1:T(8,128)(2,1)S(1)} %fusion, bf16[128,3200]{1,0:T(8,128)(2,1)S(1)} %all_gather.11), kind=kOutput, calls=%fused_computation.3 | convolution fusion | flops 657920000 | bytes 6144000 | tf_op jit(solution)/shard_map/dot_general | solution.py:61
  (59 shorter events, 0.2 us)
Async XLA Ops:
  7.2 56.3 %all-to-all-start = ((bf16[2,16,512]{2,0,1:T(2,128)(2,1)}), bf16[2,16,512]{2,0,1:T(2,128)(2,1)S(1)}, u32[]{:S(2)}, u32[]{:S(2)}) async-start(bf16[2,16,512]{2,0,1:T(2,128)(2,1)} %bitcast.46), calls=%async_computation | async-start | bytes 65536 | tf_op jit(solution)/shard_map/all_to_all | solution.py:97
  14.6 242.2 %all-reduce.4.cloned.1.call-start = ((), (), s32[]{:S(2)}) async-start(), calls=%async_computation.1 | async-start | bytes 3276800
  16.9 47.4 %copy-start.17 = (pred[32]{0:T(512)(128)(4,1)}, pred[32]{0:T(512)(128)(4,1)S(1)}, u32[]{:S(2)}) copy-start(pred[32]{0:T(512)(128)(4,1)S(1)} %compare_and_fusion) | copy-start | bytes 100
  16.9 24.6 %copy-start.24 = (s32[2,100]{1,0:T(2,128)S(1)}, s32[2,100]{1,0:T(2,128)}, u32[]{:S(2)}) copy-start(s32[2,100]{1,0:T(2,128)} %param.22) | copy-start | bytes 2404
  60.0 0.7 copy-start.23
  60.0 0.8 copy-start.11
  60.0 0.8 copy-start.21
  60.0 1.4 copy-start.19
  60.0 1.5 copy-start.1
  60.0 2.2 copy-start.26
  60.0 4.3 %copy-start.2 = (f32[12800]{0:T(1024)S(1)}, f32[12800]{0:T(1024)}, u32[]{:S(2)}) copy-start(f32[12800]{0:T(1024)} %param.23) | copy-start | bytes 153604
  60.0 4.3 %copy-start.8 = (bf16[32,512]{1,0:T(8,128)(2,1)S(1)}, bf16[32,512]{1,0:T(8,128)(2,1)}, u32[]{:S(2)}) copy-start(bf16[32,512]{1,0:T(8,128)(2,1)} %param.19) | copy-start | bytes 98308
  60.1 13.1 %copy-start.13 = (f32[32]{0:T(128)}, f32[32]{0:T(128)S(1)}, u32[]{:S(2)}) copy-start(f32[32]{0:T(128)S(1)} %broadcast_multiply_fusion.3) | copy-start | bytes 388
  60.6 12.5 %copy-start.15 = (f32[32]{0:T(128)}, f32[32]{0:T(128)S(1)}, u32[]{:S(2)}) copy-start(f32[32]{0:T(128)S(1)} %add_rsqrt_fusion.1) | copy-start | bytes 388
  61.5 2.0 copy-start.5
  64.2 8.9 %copy-start.3 = (bf16[32,512]{1,0:T(8,128)(2,1)}, bf16[32,512]{1,0:T(8,128)(2,1)S(1)}, u32[]{:S(2)}) copy-start(bf16[32,512]{1,0:T(8,128)(2,1)S(1)} %gather_fusion) | copy-start | bytes 98308
  149.3 11.7 %slice-start = ((s8[5120000]{0:T(1024)(128)(4,1)}), s8[925696]{0:T(1024)(128)(4,1)S(1)}, s32[]{:S(2)}) async-start(s8[5120000]{0:T(1024)(128)(4,1)} %bitcast.38), calls=%async_computation.2 | async-start | bytes 1851392
  150.9 6.1 %copy-start = (bf16[128,3200]{1,0:T(8,128)(2,1)S(1)}, bf16[128,3200]{1,0:T(8,128)(2,1)}, u32[]{:S(2)}) copy-start(bf16[128,3200]{1,0:T(8,128)(2,1)} %reshape.144) | copy-start | bytes 2457604
  150.9 6.1 %copy-start.12 = (f32[3200]{0:T(1024)S(1)}, f32[3200]{0:T(1024)}, u32[]{:S(2)}) copy-start(f32[3200]{0:T(1024)} %param.33) | copy-start | bytes 38404
  150.9 6.1 %copy-start.20 = (f32[800]{0:T(1024)S(1)}, f32[800]{0:T(1024)}, u32[]{:S(2)}) copy-start(f32[800]{0:T(1024)} %exponential_reduce_fusion) | copy-start | bytes 9604
  150.9 6.1 %copy-start.25 = (bf16[128,800]{0,1:T(8,128)(2,1)S(1)}, bf16[128,800]{0,1:T(8,128)(2,1)}, u32[]{:S(2)}) copy-start(bf16[128,800]{0,1:T(8,128)(2,1)} %param.26) | copy-start | bytes 614404
  150.9 10.1 %slice-start.1 = ((s8[5120000]{0:T(1024)(128)(4,1)}), s8[4194304]{0:T(1024)(128)(4,1)S(1)}, s32[]{:S(2)}) async-start(s8[5120000]{0:T(1024)(128)(4,1)} %bitcast.38), calls=%async_computation.3 | async-start | bytes 8388608
  163.3 0.8 copy-start.4
  163.3 0.8 copy-start.7
  163.3 0.8 copy-start.9
  163.3 0.8 copy-start.14
  163.3 0.8 copy-start.16
  163.3 0.8 copy-start.18
  164.1 92.6 %copy-start.6 = (f32[8,25]{0,1:T(8,128)S(1)}, f32[8,25]{0,1:T(8,128)}, u32[]{:S(2)}) copy-start(f32[8,25]{0,1:T(8,128)} %copy-done.5) | copy-start | bytes 2404
  164.1 92.6 %copy-start.10 = (f32[3200]{0:T(1024)S(1)}, f32[3200]{0:T(1024)}, u32[]{:S(2)}) copy-start(f32[3200]{0:T(1024)} %param.32) | copy-start | bytes 38404
  164.2 92.6 %copy-start.22 = (f32[8]{0:T(128)S(1)}, f32[8]{0:T(128)}, u32[]{:S(2)}) copy-start(f32[8]{0:T(128)} %add_rsqrt_fusion) | copy-start | bytes 100
Sparse Core Ops, SparseCore 0:
  163.5 93.2 all-reduce.3
where the time goes:
time: 292 us
  blocking collectives  136 us (47%)
  waiting for transfers between devices  85.6 us (29%)
  matrix products  31.9 us (11%)
  between operations  15.1 us (5%)
  other arithmetic  8.98 us (3%)
  starting transfers between devices  7.44 us (3%)
  local copies, waits for them, and re-layouts  6.46 us (2%)
    unnamed x2, waiting for transfers between devices  85.6 us
    psum x1, blocking collectives, body(): lax.psum(merged_gradient_term, 'dtp').astype(brain_float_half)  72.9 us
    all_gather x1, blocking collectives, body(): lax.all_gather(projector_norm_input_codes, 'dtp', axis=0, tiled=True)  24.3 us
    all_gather x1, blocking collectives, body(): lax.all_gather(mid_normed, 'dtp', axis=0, tiled=True)  21.8 us
    all_gather x1, blocking collectives, body(): lax.all_gather(projector_norm_input_exponents, 'dtp', axis=0, tiled=True)  17.5 us
    dot_general x3, matrix products, contract_rows(): lax.dot_general(left, right, (((0,), (0,)), ((), ())), preferred_element_...  16.9 us
    dot_general x3, matrix products, contract_cols(): lax.dot_general(left, right, (((1,), (1,)), ((), ())), preferred_element_...  15 us
    all_to_all x1, starting transfers between devices, body(): lax.all_to_all(grad_dec, 'dtp', split_axis=1, concat_axis=0, tiled=True)  7.4 us
  transfers between devices with their start and end apart: 2, of which 1 were waited for; matrix products, arithmetic and copies ran while one was open for 4% of the time, Pallas kernels for 0%

commit v1 on v0

--- a/solution.py
+++ b/solution.py
@@ -3,6 +3,8 @@
 import jax
 import jax.numpy as jnp
 from jax import lax
+from jax.experimental import pallas as pl
+from jax.experimental.pallas import tpu as pltpu
 from jax.sharding import PartitionSpec as P
 
 
@@ -140,9 +142,412 @@
     return (grad_proj_weight, grad_vit_down, grad_vit_up, grad_vit_in)
 
 
+FT = 640
+
+
+def fused_kernel(
+    gdec, tok, pp, mloc, gain, bias, pre_t, mid, mgain, lscale, w_h, vd_h, vu_h,
+    gpw_h, gvd_h, gvu_h, gvin,
+    wv, vdv, vuv, recv, mall, midall, goall, part, rc, ry, rz, sy, sz, acc, scr, nat,
+    br, gp, gact, gvp_t, hid_t, gg_t, mu, rsd, stat, lsem, osem, ss, rsem,
+):
+    f32, b16 = jnp.float32, jnp.bfloat16
+    d = lax.axis_index("dtp")
+    z, y, c = d // 4, (d // 2) % 2, d % 2
+    q_own = 2 * y + c
+    core_peer, y_peer = d + 1 - 2 * c, d + 2 - 4 * y
+    width = gp.shape[1]
+    qw = nat.shape[1]
+    tiles = qw // FT
+    features = scr.shape[1]
+    counter = [0]
+    sent = []
+
+    def sem_ids(n):
+        counter[0] += n
+        return counter[0] - n
+
+    def copy(src, dst, i, peer):
+        return pltpu.make_async_remote_copy(
+            src_ref=src, dst_ref=dst, send_sem=ss.at[i], recv_sem=rsem.at[i],
+            device_id={"dtp": peer}, device_id_type=pl.DeviceIdType.MESH,
+        )
+
+    def send(src, dst, i, peer):
+        one = copy(src, dst, i, peer)
+        one.start()
+        sent.append(one)
+
+    def lanes(t, base=0, size=FT):
+        return pl.ds(pl.multiple_of(base + t * size, 128), size)
+
+    order = [1 - c, 3 - c, 2 * (1 - y) + c, q_own]
+    w_in = []
+    for i, q in enumerate(order):
+        rows = pl.ds(pl.multiple_of(q * qw, 128), qw)
+        one = pltpu.make_async_copy(w_h.at[rows, :], wv.at[rows, :], lsem.at[i])
+        one.start()
+        w_in.append(one)
+    vd_in = pltpu.make_async_copy(vd_h, vdv, lsem.at[4])
+    vu_in = pltpu.make_async_copy(vu_h, vuv, lsem.at[5])
+    vd_in.start()
+    vu_in.start()
+
+    barrier = pltpu.get_barrier_semaphore()
+    for k in range(1, 16):
+        pl.semaphore_signal(
+            barrier, inc=1, device_id={"dtp": (d + k) % 16},
+            device_id_type=pl.DeviceIdType.MESH,
+        )
+    pl.semaphore_wait(barrier, 15)
+
+    class Gather:
+        def __init__(self, buf):
+            self.buf, self.base = buf, sem_ids(16)
+
+        def go(self, owner, i, peer):
+            send(self.buf.at[owner], self.buf.at[owner], self.base + i, peer)
+
+        def arrive(self, owner, i):
+            copy(self.buf.at[owner], self.buf.at[owner], self.base + i, core_peer).wait_recv()
+
+        def start(self):
+            for k in (1, 2, 3):
+                self.go(d, k - 1, (z + k) % 4 * 4 + q_own)
+            self.go(d, 3, y_peer)
+            self.go(d, 7, core_peer)
+
+        def forward_z(self):
+            for k in (1, 3, 2):
+                owner = (z + 4 - k) % 4 * 4 + q_own
+                self.arrive(owner, k - 1)
+                self.go(owner, 3 + k, y_peer)
+                self.go(owner, 7 + k, core_peer)
+
+        def forward_y(self):
+            for k in (0, 1, 3, 2):
+                owner = (z + 4 - k) % 4 * 4 + 2 * (1 - y) + c
+                self.arrive(owner, 3 + k)
+                self.go(owner, 11 + k, core_peer)
+
+        def finish(self):
+            for k in range(4):
+                self.arrive((z + 4 - k) % 4 * 4 + 2 * y + 1 - c, 7 + k)
+            for k in range(4):
+                self.arrive((z + 4 - k) % 4 * 4 + 2 * (1 - y) + 1 - c, 11 + k)
+
+    class Scatter:
+        def __init__(self, r):
+            self.r, self.base = r, sem_ids(6)
+
+        def core(self, yy):
+            send(part.at[self.r, 2 * yy + 1 - c], rc.at[self.r, yy], self.base + yy, core_peer)
+
+        def core_wait(self, yy, i):
+            copy(part.at[self.r, 2 * yy + 1 - c], rc.at[self.r, yy], self.base + i, core_peer).wait_recv()
+
+        def middle(self):
+            r = self.r
+
+            @pl.loop(0, tiles)
+            def _(t):
+                s = lanes(t)
+                sy[r, :, :, s] = (
+                    part[r, 2 * (1 - y) + c, :, :, s].astype(f32)
+                    + rc[r, 1 - y, :, :, s].astype(f32)
+                ).astype(b16)
+
+            send(sy.at[r], ry.at[r], self.base + 2, y_peer)
+
+        def last(self):
+            r = self.r
+            copy(sy.at[r], ry.at[r], self.base + 2, y_peer).wait_recv()
+
+            @pl.loop(0, tiles)
+            def _(t):
+                s = lanes(t)
+                acc[:, :, s] = (
+                    part[r, q_own, :, :, s].astype(f32) + rc[r, y, :, :, s].astype(f32)
+                    + ry[r, :, :, s].astype(f32)
+                )
+
+            for k in (2, 1, 3):
+                sz[r, k - 1] = acc[(z + k) % 4].astype(b16)
+                send(sz.at[r, k - 1], rz.at[r, k - 1], self.base + 2 + k, (z + k) % 4 * 4 + q_own)
+
+        def finish(self):
+            r = self.r
+            for k in (1, 2, 3):
+                copy(sz.at[r, k - 1], rz.at[r, k - 1], self.base + 2 + k, core_peer).wait_recv()
+            return (
+                acc[z] + rz[r, 0].astype(f32) + rz[r, 1].astype(f32) + rz[r, 2].astype(f32)
+            )
+
+    a2a = sem_ids(16)
+
+    def own_columns(p):
+        return pl.ds(pl.multiple_of(p * width, 128), width)
+
+    for k in range(1, 16):
+        p = (d + k) % 16
+        send(gdec.at[:, own_columns(p)], recv.at[d], a2a + k, p)
+    mall[d] = mloc[...]
+    g_in = Gather(mall)
+    g_in.start()
+    recv[d] = gdec[:, own_columns(d)]
+    proj_grad = gelu_grad(pp[...].astype(f32))
+    for k in range(1, 16):
+        p = (d + 16 - k) % 16
+        copy(recv.at[p], recv.at[p], a2a + k, p).wait_recv()
+    for i in range(16):
+        gact[2 * i : 2 * i + 2, :] = recv[i].astype(f32)
+    place = (lax.broadcasted_iota(jnp.int32, (32, 32), 0) == tok[...]).astype(f32).astype(b16)
+    grad_act = jnp.dot(place, gact[...].astype(b16), preferred_element_type=f32)
+    gp[...] = (grad_act * proj_grad).astype(b16)
+
+    s1 = Scatter(0)
+
+    def project(i):
+        q = order[i]
+        w_in[i].wait()
+
+        @pl.loop(0, tiles)
+        def _(t):
+            res = contract_cols(gp[...], wv[lanes(t, q * qw), :])
+            part[0, q, :, :, lanes(t)] = res.reshape(4, 8, FT).astype(b16)
+
+    project(0)
+    s1.core(0)
+    project(1)
+    s1.core(1)
+    g_in.forward_z()
+    project(2)
+    project(3)
+    g_in.forward_y()
+    s1.core_wait(0, 0)
+    s1.core_wait(1, 1)
+    s1.middle()
+
+    def rms(t):
+        s = lanes(t)
+        v = mid[:, s].astype(f32)
+        return jnp.sum(v * v, axis=-1, keepdims=True)
+
+    rms_sum = lax.fori_loop(0, tiles, lambda t, a: a + rms(t), jnp.zeros((8, 1), f32))
+    recip = lax.rsqrt(rms_sum / qw + 1e-06)
+
+    @pl.loop(0, tiles)
+    def _(t):
+        s = lanes(t)
+        midall[d, :, s] = (mid[:, s].astype(f32) * recip * mgain[:, s]).astype(b16)
+
+    s1.last()
+    g_mid = Gather(midall)
+    g_mid.start()
+
+    g_in.finish()
+    all_tiles = features // FT
+    zero = jnp.zeros((32, 1), f32)
+
+    def mean_step(t, a):
+        s = lanes(t)
+        for i in range(16):
+            scr[2 * i : 2 * i + 2, s] = mall[i, :, s].astype(f32)
+        return a + jnp.sum(scr[:, s], axis=-1, keepdims=True)
+
+    mean = lax.fori_loop(0, all_tiles, mean_step, zero) / features
+
+    def var_step(t, a):
+        s = lanes(t)
+        center = scr[:, s] - mean
+        scr[:, s] = center
+        return a + jnp.sum(center * center, axis=-1, keepdims=True)
+
+    variance = lax.fori_loop(0, all_tiles, var_step, zero) / features
+    rsd[...] = jnp.broadcast_to(lax.rsqrt(variance + 1e-05), rsd.shape)
+
+    total = s1.finish()
+    own_rows = pl.ds(pl.multiple_of(z * 8, 8), 8)
+    own_lanes = pl.ds(pl.multiple_of(q_own * qw, 128), qw)
+    rstd8 = rsd[own_rows, 0:1]
+    gy = total * gain[:, own_lanes]
+    xh = scr[own_rows, own_lanes] * rstd8
+    first = jnp.sum(gy, axis=-1, keepdims=True)
+    second = jnp.sum(gy * xh, axis=-1, keepdims=True)
+    lane = lax.broadcasted_iota(jnp.int32, (8, 128), 1)
+    stat[0] = jnp.where(lane < 64, first, second)
+    st = sem_ids(3)
+    plane = [core_peer, y_peer, 4 * z + 3 - q_own]
+    for j in range(3):
+        send(stat.at[0], stat.at[j + 1], st + j, plane[j])
+    for j in range(3):
+        copy(stat.at[0], stat.at[j + 1], st + j, plane[j]).wait_recv()
+    sums = (stat[0] + stat[1] + stat[2] + stat[3]) / features
+    lead, trail = sums[:, 0:1], sums[:, 64:65]
+    goall[d] = (rstd8 * (gy - lead - xh * trail)).astype(b16)
+    g_out = Gather(goall)
+    g_out.start()
+
+    outs = []
+
+    def weight_grad(h):
+        @pl.loop(0, tiles)
+        def _(t):
+            s = lanes(t, h * qw)
+            normed = (scr[:, s] * rsd[:, 0:1] * gain[:, s] + bias[:, s]).astype(b16)
+            wv[s, :] = contract_rows(normed, gp[...]).astype(b16)
+
+        rows = pl.ds(h * qw, qw)
+        one = pltpu.make_async_copy(wv.at[rows, :], gpw_h.at[rows, :], osem.at[h])
+        one.start()
+        outs.append(one)
+
+    weight_grad(0)
+    g_out.forward_z()
+    g_mid.forward_z()
+    units = 160
+
+    @pl.loop(0, vdv.shape[0] // units)
+    def _(t):
+        s = pl.ds(pl.multiple_of(t * units, 32), units)
+        v = pre_t[s, :].astype(f32)
+        cdf = 0.5 * (1.0 + lax.erf(v / math.sqrt(2.0)))
+        hid_t[s, :] = (v * cdf).astype(b16)
+        gg_t[s, :] = cdf + v * jnp.exp(-0.5 * v * v) / math.sqrt(2.0 * math.pi)
+
+    g_out.forward_y()
+    g_mid.forward_y()
+    weight_grad(1)
+    g_out.finish()
+
+    vrow = lax.broadcasted_iota(jnp.int32, (128, 128), 0)
+    held = lax.broadcasted_iota(jnp.int32, (128, 128), 1)
+    vision = held // 32 * 32 + held % 8 * 4 + held // 8 % 4
+    shuffle = (vrow == vision).astype(f32).astype(b16)
+
+    @pl.loop(0, tiles)
+    def _(t):
+        s = lanes(t)
+        block = goall[:, :, s].astype(f32).reshape(128, FT).astype(b16)
+        rows = jnp.dot(shuffle, block, preferred_element_type=f32)
+        nat[:, s] = rows
+        br[:, s] = (rows * lscale[:, s]).astype(b16)
+
+    vd_in.wait()
+
+    @pl.loop(0, vdv.shape[0] // units)
+    def _(t):
+        s = pl.ds(pl.multiple_of(t * units, 32), units)
+        gvp_t[s, :] = (contract_cols(vdv[s, :], br[...]) * gg_t[s, :]).astype(b16)
+
+    vu_in.wait()
+
+    @pl.loop(0, tiles)
+    def _(t):
+        s = lanes(t)
+        res = contract_rows(gvp_t[...], vuv[:, s]).reshape(4, 4, 8, FT)
+        for q in range(4):
+            part[1, q, :, :, s] = res[:, q].astype(b16)
+
+    s2 = Scatter(1)
+    s2.core(0)
+    s2.core(1)
+    weight_grad(2)
+    s2.core_wait(0, 0)
+    s2.core_wait(1, 1)
+    s2.middle()
+
+    @pl.loop(0, vdv.shape[0] // units)
+    def _(t):
+        s = pl.ds(pl.multiple_of(t * units, 32), units)
+        vdv[s, :] = jnp.dot(hid_t[s, :], br[...], preferred_element_type=f32).astype(b16)
+
+    one = pltpu.make_async_copy(vdv, gvd_h, osem.at[4])
+    one.start()
+    outs.append(one)
+    s2.last()
+    g_mid.finish()
+
+    @pl.loop(0, tiles)
+    def _(t):
+        s = lanes(t)
+        block = midall[:, :, s].astype(f32).reshape(128, FT).astype(b16)
+        vuv[:, s] = jnp.dot(gvp_t[...], block, preferred_element_type=f32).astype(b16)
+
+    one = pltpu.make_async_copy(vuv, gvu_h, osem.at[5])
+    one.start()
+    outs.append(one)
+    weight_grad(3)
+    gn = s2.finish() * mgain[...]
+    uhat = mid[...].astype(f32) * recip
+    back = recip * (gn - uhat * jnp.mean(gn * uhat, axis=-1, keepdims=True))
+    gvin[...] = (nat[pl.ds(pl.multiple_of(d * 8, 8), 8), :] + back).astype(b16)
+    for one in sent:
+        one.wait_send()
+    for one in outs:
+        one.wait()
+
+
+def fused_body(
+    grad_dec, token_order, proj_pre_codes, proj_pre_exps, projector_norm_input_codes,
+    projector_norm_input_exponents, projector_norm_gain, projector_norm_bias, proj_weight,
+    vit_pre_codes, vit_pre_exps, vit_down, vit_up, vit_mid_codes, vit_mid_exps, mid_gain,
+    layer_scale,
+):
+    f32, b16 = jnp.float32, jnp.bfloat16
+    merged = decode_block_columns(
+        projector_norm_input_codes, projector_norm_input_exponents
+    ).astype(b16)
+    mid = decode_block_columns(vit_mid_codes, vit_mid_exps).astype(b16)
+    pre_t = dequant_rows(vit_pre_codes, vit_pre_exps).astype(b16).T
+    proj_pre = decode_block_columns(proj_pre_codes, proj_pre_exps).astype(b16)
+    features, width = proj_weight.shape
+    units, d_vit = vit_down.shape
+    vmem = pl.BlockSpec(memory_space=pltpu.VMEM)
+    hbm = pl.BlockSpec(memory_space=pl.ANY)
+    scratch = [
+        ((features, width), b16), ((units, d_vit), b16), ((units, d_vit), b16),
+        ((16, 2, width), b16), ((16, 2, features), b16), ((16, 8, d_vit), b16),
+        ((16, 8, d_vit), b16), ((2, 4, 4, 8, d_vit), b16), ((2, 2, 4, 8, d_vit), b16),
+        ((2, 4, 8, d_vit), b16), ((2, 3, 8, d_vit), b16), ((2, 4, 8, d_vit), b16),
+        ((2, 3, 8, d_vit), b16), ((4, 8, d_vit), f32), ((32, features), f32),
+        ((128, d_vit), f32), ((128, d_vit), b16), ((32, width), b16), ((32, width), f32),
+        ((units, 128), b16), ((units, 128), b16), ((units, 128), f32), ((32, 128), f32),
+        ((32, 128), f32), ((4, 8, 128), f32),
+    ]
+    gpw, gvd, gvu, gvin = pl.pallas_call(
+        fused_kernel,
+        out_shape=(
+            jax.ShapeDtypeStruct((features, width), b16),
+            jax.ShapeDtypeStruct((units, d_vit), b16),
+            jax.ShapeDtypeStruct((units, d_vit), b16),
+            jax.ShapeDtypeStruct((8, d_vit), b16),
+        ),
+        in_specs=[vmem] * 10 + [hbm] * 3,
+        out_specs=(hbm, hbm, hbm, vmem),
+        scratch_shapes=[pltpu.VMEM(s, t) for s, t in scratch]
+        + [
+            pltpu.SemaphoreType.DMA((6,)), pltpu.SemaphoreType.DMA((6,)),
+            pltpu.SemaphoreType.DMA((80,)), pltpu.SemaphoreType.DMA((80,)),
+        ],
+        compiler_params=pltpu.CompilerParams(
+            collective_id=0, has_side_effects=True, vmem_limit_bytes=60 * 2**20
+        ),
+        cost_estimate=pl.CostEstimate(
+            flops=3 * 10**9, bytes_accessed=48 * 10**6, transcendentals=2 * 10**5
+        ),
+    )(
+        grad_dec, token_order.reshape(1, -1), proj_pre, merged,
+        projector_norm_gain.reshape(1, -1), projector_norm_bias.reshape(1, -1), pre_t, mid,
+        mid_gain.reshape(1, -1), layer_scale.reshape(1, -1), proj_weight, vit_down, vit_up.T,
+    )
+    return gpw, gvd, gvu.T, gvin
+
+
 def solution(mesh):
+    fused = mesh.shape["dtp"] == 16
     return jax.shard_map(
-        body,
+        fused_body if fused else body,
         mesh=mesh,
         in_specs=(
             P(("groups", "dtp"), None),

time: 292 us -> 108 us (0.37)
  blocking collectives: 136 us -> 0 us
  waiting for transfers between devices: 85.6 us -> 0 us
  Pallas kernels: 0 us -> 73 us
  matrix products: 31.9 us -> 0 us
  local copies, waits for them, and re-layouts: 6.46 us -> 24.4 us
  between operations: 15.1 us -> 0.68 us
  starting transfers between devices: 7.44 us -> 0 us
    unnamed x2 -> x0, waiting for transfers between devices: 85.6 us -> none
    pallas_call x0 -> x1, Pallas kernels: none -> 73 us  [fused_body(): pl.pallas_call(fused_kernel, out_shape=(jax.ShapeDtypeStruct((features, w...]
    psum x1 -> x0, blocking collectives: 72.9 us -> none  [body(): lax.psum(merged_gradient_term, 'dtp').astype(brain_float_half)]
    all_gather x3 -> x0, blocking collectives: 63.6 us -> none  [the longest x1 24.3 us: body(): lax.all_gather(projector_norm_input_codes, 'dtp', axis=0, tiled=True)]
    dot_general x6 -> x0, matrix products: 31.9 us -> none  [the longest x3 16.9 us: contract_rows(): lax.dot_general(left, right, (((0,), (0,)), ((), ())), preferred_element_...]
    unnamed x59 -> x11, local copies, waits for them, and re-layouts: 1.67 us -> 18.5 us
    all_to_all x1 -> x0, starting transfers between devices: 7.4 us -> none  [body(): lax.all_to_all(grad_dec, 'dtp', split_axis=1, concat_axis=0, tiled=True)]
    reshape x1 -> x4, local copies, waits for them, and re-layouts: 1.56 us -> 5.58 us  [the longest x1 1.46 us: fused_body(): projector_norm_gain.reshape(1, -1)]
  transfers between devices with their start and end apart: 2 -> 0, of which waited for: 1 -> 0; matrix products, arithmetic and copies ran while one was open for 4% -> 0% of each run, Pallas kernels for 0% -> 0%
where the time goes in v1:
time: 108 us; the launch traced here: 107 us
  Pallas kernels  73 us (68%)
  local copies, waits for them, and re-layouts  24.4 us (23%)
  other arithmetic  8.95 us (8%)
    pallas_call x1, Pallas kernels, fused_body(): pl.pallas_call(fused_kernel, out_shape=(jax.ShapeDtypeStruct((features, w...  73 us
    unnamed x11, local copies, waits for them, and re-layouts  18.5 us

profile of v1, /device:TPU:0, one launch (start us, length us, event | category | flops | bytes accessed | tf_op | source)
XLA Modules:
  0.0 107.0 jit_solution(15596154262487494249)
XLA Ops:
  0.6 0.7 multiply_exponential_fusion.2
  1.3 0.7 multiply_exponential_fusion.1
  2.0 0.7 exponential_reduce_fusion
  2.7 0.7 multiply_exponential_fusion
  3.4 0.1 copy.24
  3.5 1.3 %reshape.45.mgain = f32[1,3200]{1,0:T(1,128)} reshape(f32[3200]{0:T(1024)} %param.32) | data formatting | bytes 25600 | tf_op jit(solution)/shard_map/reshape | solution.py:542
  4.8 1.3 %reshape.46.lscale = f32[1,3200]{1,0:T(1,128)} reshape(f32[3200]{0:T(1024)} %param.33) | data formatting | bytes 25600 | tf_op jit(solution)/shard_map/reshape | solution.py:542
  6.2 0.1 copy.23
  6.2 1.5 %fusion.2.mid = bf16[8,3200]{1,0:T(8,128)(2,1)} fusion(bf16[8,3200]{1,0:T(8,128)(2,1)} %param.30, f32[8,25]{0,1:T(8,128)S(1)} %copy.24), kind=kLoop, calls=%fused_computation.5 | loop fusion | flops 76800 | bytes 103200 | tf_op jit(solution)/shard_map/convert_element_type | solution.py:501
  7.8 0.1 mul.44
  7.9 1.4 %fusion.3.pp = bf16[32,512]{1,0:T(8,128)(2,1)} fusion(f32[4,8,4,128]{3,2,1,0:T(4,128)S(1)} %bitcast.22, bf16[32,512]{1,0:T(8,128)(2,1)} %param.19), kind=kLoop, calls=%fused_computation.7 | loop fusion | flops 49152 | bytes 131072 | tf_op jit(solution)/shard_map/convert_element_type | solution.py:503
  9.2 1.5 %reshape.43.gain = f32[1,12800]{1,0:T(1,128)} reshape(f32[12800]{0:T(1024)} %param.23) | data formatting | bytes 102400 | tf_op jit(solution)/shard_map/reshape | solution.py:541
  10.7 1.5 %reshape.44.bias = f32[1,12800]{1,0:T(1,128)} reshape(f32[12800]{0:T(1024)} %param.24) | data formatting | bytes 102400 | tf_op jit(solution)/shard_map/reshape | solution.py:541
  12.2 0.1 broadcast_bitcast_fusion
  12.2 1.5 %fusion.1.mloc = bf16[2,12800]{1,0:T(2,128)(2,1)} fusion(f32[1,2,100,128]{3,2,1,0:T(8,128)S(1)} %broadcast_bitcast_fusion, bf16[2,12800]{1,0:T(2,128)(2,1)} %param.21), kind=kLoop, calls=%fused_computation.3 | loop fusion | flops 76800 | bytes 204800 | tf_op jit(solution)/shard_map/convert_element_type | solution.py:500
  13.7 1.8 %fusion.pre_t = bf16[800,128]{1,0:T(8,128)(2,1)} fusion(bf16[128,800]{0,1:T(8,128)(2,1)} %param.26, f32[800]{0:T(1024)S(1)} %exponential_reduce_fusion), kind=kLoop, calls=%fused_computation.1 | loop fusion | flops 307200 | bytes 412800 | tf_op jit(solution)/shard_map/transpose | solution.py:502
  15.5 73.0 %shard_map.192 = (bf16[12800,512]{1,0:T(8,128)(2,1)}, bf16[800,3200]{1,0:T(8,128)(2,1)}, bf16[800,3200]{1,0:T(8,128)(2,1)}, bf16[8,3200]{1,0:T(8,128)(2,1)}) custom-call(bf16[2,8192]{1,0:T(2,128)(2,1)} %gdec.1, s32[1,32]{1,0:T(1,128)} %bitcast.23, bf16[32,512]{1,0:T(8,128)(2,1)} %fusion.3.pp, bf16[2,12800]{1,0:T(2,128)(2,1)} %fusion.1.mloc, ...), custom_call_target="tpu_custom_call" | custom-call | flops 3000000000 | bytes 48000000 | tf_op jit(solution)/shard_map/pallas_call | solution.py:518
  88.5 0.0 copy-start.1
  88.6 11.2 %copy.33 = bf16[12800,512]{1,0:T(8,128)(2,1)} copy(bf16[12800,512]{1,0:T(8,128)(2,1)} %get-tuple-element.16) | data formatting | bytes 26214400
  99.8 0.0 copy-done.1
  99.8 0.0 copy-start
  99.8 2.6 %copy.34 = bf16[800,3200]{1,0:T(8,128)(2,1)} copy(bf16[800,3200]{1,0:T(8,128)(2,1)S(1)} %copy-done.1) | data formatting | bytes 10240000
  102.4 1.7 %copy-done = bf16[800,3200]{1,0:T(8,128)(2,1)S(1)} copy-done((bf16[800,3200]{1,0:T(8,128)(2,1)S(1)}, bf16[800,3200]{1,0:T(8,128)(2,1)}, u32[]{:S(2)}) %copy-start) | copy-done | bytes 5120024
  104.1 0.0 copy-start.2
  104.1 2.3 %copy.35 = bf16[3200,800]{0,1:T(8,128)(2,1)} copy(bf16[3200,800]{0,1:T(8,128)(2,1)S(1)} %bitcast.20) | data formatting | bytes 10240000
  106.4 0.0 copy-done.2
  106.4 0.6 copy.36
Async XLA Ops:
  88.5 11.2 %copy-start.1 = (bf16[800,3200]{1,0:T(8,128)(2,1)S(1)}, bf16[800,3200]{1,0:T(8,128)(2,1)}, u32[]{:S(2)}) copy-start(bf16[800,3200]{1,0:T(8,128)(2,1)} %get-tuple-element.17) | copy-start | bytes 15360004
  99.8 4.3 %copy-start = (bf16[800,3200]{1,0:T(8,128)(2,1)S(1)}, bf16[800,3200]{1,0:T(8,128)(2,1)}, u32[]{:S(2)}) copy-start(bf16[800,3200]{1,0:T(8,128)(2,1)} %get-tuple-element.10) | copy-start | bytes 15360004
  104.1 2.3 %copy-start.2 = (bf16[8,3200]{1,0:T(8,128)(2,1)S(1)}, bf16[8,3200]{1,0:T(8,128)(2,1)}, u32[]{:S(2)}) copy-start(bf16[8,3200]{1,0:T(8,128)(2,1)} %get-tuple-element.19) | copy-start | bytes 153604

commit v2 on v1

--- a/solution.py
+++ b/solution.py
@@ -143,13 +143,15 @@
 
 
 FT = 640
+BLOCK = 128
 
 
 def fused_kernel(
-    gdec, tok, pp, mloc, gain, bias, pre_t, mid, mgain, lscale, w_h, vd_h, vu_h,
-    gpw_h, gvd_h, gvu_h, gvin,
+    gdec, tok, ppc, ppe, mlc, mle, gain2, bias2, pre_c, pre_e, midc, mide, mgain2, lscale2,
+    w_h, vd_h, vu_h,
+    normed, gp, hid_t, br, gvp_t, midn, gvin,
     wv, vdv, vuv, recv, mall, midall, goall, part, rc, ry, rz, sy, sz, acc, scr, nat,
-    br, gp, gact, gvp_t, hid_t, gg_t, mu, rsd, stat, lsem, osem, ss, rsem,
+    gact, gg_t, pre_t, mid, gain, bias, mgain, lscale, rsd, stat, lsem, ss, rsem,
 ):
     f32, b16 = jnp.float32, jnp.bfloat16
     d = lax.axis_index("dtp")
@@ -291,11 +293,21 @@
     for k in range(1, 16):
         p = (d + k) % 16
         send(gdec.at[:, own_columns(p)], recv.at[d], a2a + k, p)
-    mall[d] = mloc[...]
+    mscale = jnp.exp2((mle[...] - 8).astype(f32))
+    for j in range(features // BLOCK):
+        s = pl.ds(j * BLOCK, BLOCK)
+        mall[d, :, s] = (mlc[:, s].astype(f32) * mscale[:, j : j + 1]).astype(b16)
     g_in = Gather(mall)
     g_in.start()
     recv[d] = gdec[:, own_columns(d)]
-    proj_grad = gelu_grad(pp[...].astype(f32))
+    pscale = jnp.exp2((ppe[...] - 8).astype(f32))
+    proj_grad = jnp.concatenate(
+        [
+            gelu_grad(ppc[:, BLOCK * j : BLOCK * (j + 1)].astype(f32) * pscale[:, j : j + 1])
+            for j in range(width // BLOCK)
+        ],
+        axis=1,
+    )
     for k in range(1, 16):
         p = (d + 16 - k) % 16
         copy(recv.at[p], recv.at[p], a2a + k, p).wait_recv()
@@ -328,9 +340,17 @@
     s1.core_wait(1, 1)
     s1.middle()
 
+    for flat, line in ((gain2, gain), (bias2, bias), (mgain2, mgain), (lscale2, lscale)):
+        for j in range(flat.shape[0]):
+            line[:, BLOCK * j : BLOCK * (j + 1)] = flat[j : j + 1, :]
+    dscale = jnp.exp2((mide[...] - 8).astype(f32))
+    for j in range(qw // BLOCK):
+        s = pl.ds(j * BLOCK, BLOCK)
+        mid[:, s] = midc[:, s].astype(f32) * dscale[:, j : j + 1]
+
     def rms(t):
         s = lanes(t)
-        v = mid[:, s].astype(f32)
+        v = mid[:, s]
         return jnp.sum(v * v, axis=-1, keepdims=True)
 
     rms_sum = lax.fori_loop(0, tiles, lambda t, a: a + rms(t), jnp.zeros((8, 1), f32))
@@ -339,7 +359,7 @@
     @pl.loop(0, tiles)
     def _(t):
         s = lanes(t)
-        midall[d, :, s] = (mid[:, s].astype(f32) * recip * mgain[:, s]).astype(b16)
+        midall[d, :, s] = (mid[:, s] * recip * mgain[:, s]).astype(b16)
 
     s1.last()
     g_mid = Gather(midall)
@@ -388,36 +408,21 @@
     g_out = Gather(goall)
     g_out.start()
 
-    outs = []
-
-    def weight_grad(h):
-        @pl.loop(0, tiles)
-        def _(t):
-            s = lanes(t, h * qw)
-            normed = (scr[:, s] * rsd[:, 0:1] * gain[:, s] + bias[:, s]).astype(b16)
-            wv[s, :] = contract_rows(normed, gp[...]).astype(b16)
-
-        rows = pl.ds(h * qw, qw)
-        one = pltpu.make_async_copy(wv.at[rows, :], gpw_h.at[rows, :], osem.at[h])
-        one.start()
-        outs.append(one)
-
-    weight_grad(0)
     g_out.forward_z()
-    g_mid.forward_z()
+    spread = jnp.broadcast_to(jnp.exp2((pre_e[...] - 8).astype(f32)) / 16, (16, vdv.shape[0]))
+    pre_t[...] = contract_rows(spread.astype(b16), jnp.ones((16, 128), b16))
     units = 160
 
     @pl.loop(0, vdv.shape[0] // units)
     def _(t):
         s = pl.ds(pl.multiple_of(t * units, 32), units)
-        v = pre_t[s, :].astype(f32)
+        v = pre_c[s, :].astype(f32) * pre_t[s, :]
         cdf = 0.5 * (1.0 + lax.erf(v / math.sqrt(2.0)))
         hid_t[s, :] = (v * cdf).astype(b16)
         gg_t[s, :] = cdf + v * jnp.exp(-0.5 * v * v) / math.sqrt(2.0 * math.pi)
 
     g_out.forward_y()
-    g_mid.forward_y()
-    weight_grad(1)
+    g_mid.forward_z()
     g_out.finish()
 
     vrow = lax.broadcasted_iota(jnp.int32, (128, 128), 0)
@@ -452,40 +457,48 @@
     s2 = Scatter(1)
     s2.core(0)
     s2.core(1)
-    weight_grad(2)
+    g_mid.forward_y()
     s2.core_wait(0, 0)
     s2.core_wait(1, 1)
     s2.middle()
 
-    @pl.loop(0, vdv.shape[0] // units)
+    @pl.loop(0, features // FT)
     def _(t):
-        s = pl.ds(pl.multiple_of(t * units, 32), units)
-        vdv[s, :] = jnp.dot(hid_t[s, :], br[...], preferred_element_type=f32).astype(b16)
-
-    one = pltpu.make_async_copy(vdv, gvd_h, osem.at[4])
-    one.start()
-    outs.append(one)
+        s = lanes(t)
+        normed[:, s] = (scr[:, s] * rsd[:, 0:1] * gain[:, s] + bias[:, s]).astype(b16)
+
     s2.last()
     g_mid.finish()
 
     @pl.loop(0, tiles)
     def _(t):
         s = lanes(t)
-        block = midall[:, :, s].astype(f32).reshape(128, FT).astype(b16)
-        vuv[:, s] = jnp.dot(gvp_t[...], block, preferred_element_type=f32).astype(b16)
-
-    one = pltpu.make_async_copy(vuv, gvu_h, osem.at[5])
-    one.start()
-    outs.append(one)
-    weight_grad(3)
+        midn[:, s] = midall[:, :, s].astype(f32).reshape(128, FT).astype(b16)
+
     gn = s2.finish() * mgain[...]
-    uhat = mid[...].astype(f32) * recip
+    uhat = mid[...] * recip
     back = recip * (gn - uhat * jnp.mean(gn * uhat, axis=-1, keepdims=True))
     gvin[...] = (nat[pl.ds(pl.multiple_of(d * 8, 8), 8), :] + back).astype(b16)
     for one in sent:
         one.wait_send()
-    for one in outs:
-        one.wait()
+
+
+def weights_kernel(normed, gp, hid_t, br, gvp_t, midn, gvin, gpw, gvd, gvu, out):
+    f32, b16 = jnp.float32, jnp.bfloat16
+    step = pl.program_id(0)
+    gpw[...] = contract_rows(normed[...], gp[...]).astype(b16)
+
+    @pl.when(step % 5 == 0)
+    def _():
+        gvd[...] = jnp.dot(hid_t[...], br[...], preferred_element_type=f32).astype(b16)
+
+    @pl.when(step % 5 == 2)
+    def _():
+        gvu[...] = jnp.dot(gvp_t[...], midn[...], preferred_element_type=f32).astype(b16)
+
+    @pl.when(step == 0)
+    def _():
+        out[...] = gvin[...]
 
 
 def fused_body(
@@ -495,12 +508,6 @@
     layer_scale,
 ):
     f32, b16 = jnp.float32, jnp.bfloat16
-    merged = decode_block_columns(
-        projector_norm_input_codes, projector_norm_input_exponents
-    ).astype(b16)
-    mid = decode_block_columns(vit_mid_codes, vit_mid_exps).astype(b16)
-    pre_t = dequant_rows(vit_pre_codes, vit_pre_exps).astype(b16).T
-    proj_pre = decode_block_columns(proj_pre_codes, proj_pre_exps).astype(b16)
     features, width = proj_weight.shape
     units, d_vit = vit_down.shape
     vmem = pl.BlockSpec(memory_space=pltpu.VMEM)
@@ -510,37 +517,66 @@
         ((16, 2, width), b16), ((16, 2, features), b16), ((16, 8, d_vit), b16),
         ((16, 8, d_vit), b16), ((2, 4, 4, 8, d_vit), b16), ((2, 2, 4, 8, d_vit), b16),
         ((2, 4, 8, d_vit), b16), ((2, 3, 8, d_vit), b16), ((2, 4, 8, d_vit), b16),
-        ((2, 3, 8, d_vit), b16), ((4, 8, d_vit), f32), ((32, features), f32),
-        ((128, d_vit), f32), ((128, d_vit), b16), ((32, width), b16), ((32, width), f32),
-        ((units, 128), b16), ((units, 128), b16), ((units, 128), f32), ((32, 128), f32),
-        ((32, 128), f32), ((4, 8, 128), f32),
+        ((2, 3, 8, d_vit), b16), ((4, 8, d_vit), f32),
+        ((32, features), f32), ((128, d_vit), f32), ((32, width), f32),
+        ((units, 128), f32), ((units, 128), f32), ((8, d_vit), f32), ((1, features), f32),
+        ((1, features), f32), ((1, d_vit), f32), ((1, d_vit), f32), ((32, 128), f32),
+        ((4, 8, 128), f32),
     ]
+    outs = [(32, features), (32, width), (units, 128), (128, d_vit), (units, 128), (128, d_vit), (8, d_vit)]
+    held = pl.pallas_call(
+        fused_kernel,
+        out_shape=[jax.ShapeDtypeStruct(shape, b16) for shape in outs],
+        in_specs=[vmem] * 14 + [hbm] * 3,
+        out_specs=[vmem] * len(outs),
+        scratch_shapes=[pltpu.VMEM(s, t) for s, t in scratch]
+        + [
+            pltpu.SemaphoreType.DMA((6,)), pltpu.SemaphoreType.DMA((80,)),
+            pltpu.SemaphoreType.DMA((80,)),
+        ],
+        compiler_params=pltpu.CompilerParams(
+            collective_id=0, has_side_effects=True, vmem_limit_bytes=58 * 2**20
+        ),
+        cost_estimate=pl.CostEstimate(
+            flops=2 * 10**9, bytes_accessed=24 * 10**6, transcendentals=2 * 10**5
+        ),
+    )(
+        grad_dec, token_order.reshape(1, -1), proj_pre_codes, proj_pre_exps,
+        projector_norm_input_codes, projector_norm_input_exponents,
+        projector_norm_gain.reshape(-1, BLOCK), projector_norm_bias.reshape(-1, BLOCK),
+        vit_pre_codes.T, vit_pre_exps, vit_mid_codes, vit_mid_exps,
+        mid_gain.reshape(-1, BLOCK), layer_scale.reshape(-1, BLOCK), proj_weight, vit_down,
+        vit_up.T,
+    )
+    steps = 25
+    whole = lambda i: (0, 0)
+    fifth = lambda i: (0, i // 5)
     gpw, gvd, gvu, gvin = pl.pallas_call(
-        fused_kernel,
-        out_shape=(
+        weights_kernel,
+        grid=(steps,),
+        in_specs=[
+            pl.BlockSpec((32, features // steps), lambda i: (0, i)),
+            pl.BlockSpec((32, width), whole),
+            pl.BlockSpec((units, 128), whole),
+            pl.BlockSpec((128, FT), fifth),
+            pl.BlockSpec((units, 128), whole),
+            pl.BlockSpec((128, FT), fifth),
+            pl.BlockSpec((8, d_vit), whole),
+        ],
+        out_specs=[
+            pl.BlockSpec((features // steps, width), lambda i: (i, 0)),
+            pl.BlockSpec((units, FT), fifth),
+            pl.BlockSpec((units, FT), fifth),
+            pl.BlockSpec((8, d_vit), whole),
+        ],
+        out_shape=[
             jax.ShapeDtypeStruct((features, width), b16),
             jax.ShapeDtypeStruct((units, d_vit), b16),
             jax.ShapeDtypeStruct((units, d_vit), b16),
             jax.ShapeDtypeStruct((8, d_vit), b16),
-        ),
-        in_specs=[vmem] * 10 + [hbm] * 3,
-        out_specs=(hbm, hbm, hbm, vmem),
-        scratch_shapes=[pltpu.VMEM(s, t) for s, t in scratch]
-        + [
-            pltpu.SemaphoreType.DMA((6,)), pltpu.SemaphoreType.DMA((6,)),
-            pltpu.SemaphoreType.DMA((80,)), pltpu.SemaphoreType.DMA((80,)),
         ],
-        compiler_params=pltpu.CompilerParams(
-            collective_id=0, has_side_effects=True, vmem_limit_bytes=60 * 2**20
-        ),
-        cost_estimate=pl.CostEstimate(
-            flops=3 * 10**9, bytes_accessed=48 * 10**6, transcendentals=2 * 10**5
-        ),
-    )(
-        grad_dec, token_order.reshape(1, -1), proj_pre, merged,
-        projector_norm_gain.reshape(1, -1), projector_norm_bias.reshape(1, -1), pre_t, mid,
-        mid_gain.reshape(1, -1), layer_scale.reshape(1, -1), proj_weight, vit_down, vit_up.T,
-    )
+        compiler_params=pltpu.CompilerParams(vmem_limit_bytes=24 * 2**20),
+    )(*held)
     return gpw, gvd, gvu.T, gvin
 
 

time: 108 us -> 97.5 us (0.903)
  local copies, waits for them, and re-layouts: 24.4 us -> 8.21 us
  Pallas kernels: 73 us -> 88.2 us
  other arithmetic: 8.95 us -> 0 us
    pallas_call x1 -> x2, Pallas kernels: 73 us -> 88.2 us  [the longest x1 68.2 us: fused_body(): pl.pallas_call(fused_kernel, out_shape=[jax.ShapeDtypeStruct(shape, b16)...]
    unnamed x11 -> x15, local copies, waits for them, and re-layouts: 18.5 us -> 8.21 us
    reshape x4 -> x0, local copies, waits for them, and re-layouts: 5.58 us -> none  [the longest x1 1.46 us: fused_body(): projector_norm_gain.reshape(1, -1)]
    convert_element_type x3 -> x0, other arithmetic: 4.38 us -> none  [the longest x1 1.51 us: fused_body(): mid = decode_block_columns(vit_mid_codes, vit_mid_exps).astype(b16)]
    exp2 x4 -> x0, other arithmetic: 2.79 us -> none  [the longest x3 2.07 us: decode_block_columns(): scale = jnp.exp2((exps - 8).astype(jnp.float32))]
    transpose x1 -> x0, other arithmetic: 1.78 us -> none  [fused_body(): pre_t = dequant_rows(vit_pre_codes, vit_pre_exps).astype(b16).T]
where the time goes in v2:
time: 97.5 us; the launch traced here: 97 us
  Pallas kernels  88.2 us (90%)
  local copies, waits for them, and re-layouts  8.21 us (8%)
    pallas_call x1, Pallas kernels, fused_body(): pl.pallas_call(fused_kernel, out_shape=[jax.ShapeDtypeStruct(shape, b16)...  68.2 us
    pallas_call x1, Pallas kernels, fused_body(): pl.pallas_call(weights_kernel, grid=(steps,), in_specs=[pl.BlockSpec((32,...  19.9 us
    unnamed x15, local copies, waits for them, and re-layouts  8.21 us

profile of v2, /device:TPU:0, one launch (start us, length us, event | category | flops | bytes accessed | tf_op | source)
XLA Modules:
  0.0 97.0 jit_solution(18310105256026034579)
XLA Ops:
  0.6 1.4 %copy.21.ppe = s32[32,4]{1,0:T(8,128)} copy(s32[32,4]{0,1:T(4,128)} %param.20) | data formatting | bytes 1024 | tf_op args[3]
  2.0 68.2 %shard_map.192 = (bf16[32,12800]{1,0:T(8,128)(2,1)}, bf16[32,512]{1,0:T(8,128)(2,1)}, bf16[800,128]{1,0:T(8,128)(2,1)}, bf16[128,3200]{1,0:T(8,128)(2,1)}, bf16[...) custom-call(bf16[2,8192]{1,0:T(2,128)(2,1)} %gdec.1, s32[1,32]{1,0:T(1,128)} %bitcast.14, ...), custom_call_target="tpu_custom_call" | custom-call | flops 2000000000 | bytes 24000000 | tf_op jit(solution)/shard_map/pallas_call | solution.py:527
  70.2 0.0 copy-start
  70.2 1.1 %copy-done = bf16[32,12800]{1,0:T(8,128)(2,1)S(1)} copy-done((bf16[32,12800]{1,0:T(8,128)(2,1)S(1)}, bf16[32,12800]{1,0:T(8,128)(2,1)}, u32[]{:S(2)}) %copy-start) | copy-done | bytes 819224
  71.4 0.0 copy-start.1
  71.4 1.1 %copy-done.1 = bf16[128,3200]{1,0:T(8,128)(2,1)S(1)} copy-done((bf16[128,3200]{1,0:T(8,128)(2,1)S(1)}, bf16[128,3200]{1,0:T(8,128)(2,1)}, u32[]{:S(2)}) %copy-start.1) | copy-done | bytes 819224
  72.5 0.0 copy-start.2
  72.5 1.1 %copy-done.2 = bf16[128,3200]{1,0:T(8,128)(2,1)S(1)} copy-done((bf16[128,3200]{1,0:T(8,128)(2,1)S(1)}, bf16[128,3200]{1,0:T(8,128)(2,1)}, u32[]{:S(2)}) %copy-start.2) | copy-done | bytes 819224
  73.7 0.0 copy-start.3
  73.7 0.9 copy-done.3
  74.6 0.0 copy-start.4
  74.6 0.9 copy-done.4
  75.5 0.0 copy-start.5
  75.5 0.8 copy-done.5
  76.3 0.0 copy-start.6
  76.3 0.8 copy-done.6
  77.1 19.9 %shard_map.193 = (bf16[12800,512]{1,0:T(8,128)(2,1)}, bf16[800,3200]{1,0:T(8,128)(2,1)}, bf16[800,3200]{1,0:T(8,128)(2,1)}, bf16[8,3200]{1,0:T(8,128)(2,1)}) custom-call(bf16[32,12800]{1,0:T(8,128)(2,1)S(1)} %copy-done, bf16[32,512]{1,0:T(8,128)(2,1)S(1)} %copy-done.6, bf16[800,128]{1,0:T(8,128)(2,1)S(1)} %copy-done.3, bf16[128,3200]{1,0:T(8,128)(2,1)S(1)} %copy-done.1, ...), custom_call_target="tpu_custom_call" | custom-call | tf_op jit(solution)/shard_map/pallas_call | solution.py:554
Async XLA Ops:
  70.2 1.1 %copy-start = (bf16[32,12800]{1,0:T(8,128)(2,1)S(1)}, bf16[32,12800]{1,0:T(8,128)(2,1)}, u32[]{:S(2)}) copy-start(bf16[32,12800]{1,0:T(8,128)(2,1)} %get-tuple-element.15.normed) | copy-start | bytes 2457604
  71.4 1.1 %copy-start.1 = (bf16[128,3200]{1,0:T(8,128)(2,1)S(1)}, bf16[128,3200]{1,0:T(8,128)(2,1)}, u32[]{:S(2)}) copy-start(bf16[128,3200]{1,0:T(8,128)(2,1)} %get-tuple-element.18.br) | copy-start | bytes 2457604
  72.5 1.1 %copy-start.2 = (bf16[128,3200]{1,0:T(8,128)(2,1)S(1)}, bf16[128,3200]{1,0:T(8,128)(2,1)}, u32[]{:S(2)}) copy-start(bf16[128,3200]{1,0:T(8,128)(2,1)} %get-tuple-element.20.midn) | copy-start | bytes 2457604
  73.7 0.9 copy-start.3
  74.6 0.9 copy-start.4
  75.5 0.8 copy-start.5
  76.3 0.8 copy-start.6

commit v3 on v2

--- a/solution.py
+++ b/solution.py
@@ -149,9 +149,10 @@
 def fused_kernel(
     gdec, tok, ppc, ppe, mlc, mle, gain2, bias2, pre_c, pre_e, midc, mide, mgain2, lscale2,
     w_h, vd_h, vu_h,
-    normed, gp, hid_t, br, gvp_t, midn, gvin,
+    normed, gp, gvd_h, gvu_h, gvin,
     wv, vdv, vuv, recv, mall, midall, goall, part, rc, ry, rz, sy, sz, acc, scr, nat,
-    gact, gg_t, pre_t, mid, gain, bias, mgain, lscale, rsd, stat, lsem, ss, rsem,
+    gact, gg_t, pre_t, mid, gain, bias, mgain, lscale, rsd, stat, hid_t, br, gvp_t,
+    lsem, ss, rsem,
 ):
     f32, b16 = jnp.float32, jnp.bfloat16
     d = lax.axis_index("dtp")
@@ -192,8 +193,6 @@
         w_in.append(one)
     vd_in = pltpu.make_async_copy(vd_h, vdv, lsem.at[4])
     vu_in = pltpu.make_async_copy(vu_h, vuv, lsem.at[5])
-    vd_in.start()
-    vu_in.start()
 
     barrier = pltpu.get_barrier_semaphore()
     for k in range(1, 16):
@@ -330,10 +329,12 @@
 
     project(0)
     s1.core(0)
+    g_in.forward_z()
     project(1)
     s1.core(1)
-    g_in.forward_z()
+    vd_in.start()
     project(2)
+    vu_in.start()
     project(3)
     g_in.forward_y()
     s1.core_wait(0, 0)
@@ -363,7 +364,6 @@
 
     s1.last()
     g_mid = Gather(midall)
-    g_mid.start()
 
     g_in.finish()
     all_tiles = features // FT
@@ -408,7 +408,13 @@
     g_out = Gather(goall)
     g_out.start()
 
+    @pl.loop(0, all_tiles)
+    def _(t):
+        s = lanes(t)
+        normed[:, s] = (scr[:, s] * rsd[:, 0:1] * gain[:, s] + bias[:, s]).astype(b16)
+
     g_out.forward_z()
+    g_mid.start()
     spread = jnp.broadcast_to(jnp.exp2((pre_e[...] - 8).astype(f32)) / 16, (16, vdv.shape[0]))
     pre_t[...] = contract_rows(spread.astype(b16), jnp.ones((16, 128), b16))
     units = 160
@@ -422,8 +428,8 @@
         gg_t[s, :] = cdf + v * jnp.exp(-0.5 * v * v) / math.sqrt(2.0 * math.pi)
 
     g_out.forward_y()
+    g_out.finish()
     g_mid.forward_z()
-    g_out.finish()
 
     vrow = lax.broadcasted_iota(jnp.int32, (128, 128), 0)
     held = lax.broadcasted_iota(jnp.int32, (128, 128), 1)
@@ -458,45 +464,48 @@
     s2.core(0)
     s2.core(1)
     g_mid.forward_y()
+
+    def down_grad(first, count):
+        @pl.loop(first, first + count)
+        def _(t):
+            s = pl.ds(pl.multiple_of(t * units, 32), units)
+            vdv[s, :] = jnp.dot(hid_t[s, :], br[...], preferred_element_type=f32).astype(b16)
+
+    down_grad(0, 2)
     s2.core_wait(0, 0)
     s2.core_wait(1, 1)
     s2.middle()
 
-    @pl.loop(0, features // FT)
-    def _(t):
-        s = lanes(t)
-        normed[:, s] = (scr[:, s] * rsd[:, 0:1] * gain[:, s] + bias[:, s]).astype(b16)
-
+    down_grad(2, 3)
+    vd_out = pltpu.make_async_copy(vdv, gvd_h, lsem.at[4])
+    vd_out.start()
     s2.last()
     g_mid.finish()
 
     @pl.loop(0, tiles)
     def _(t):
         s = lanes(t)
-        midn[:, s] = midall[:, :, s].astype(f32).reshape(128, FT).astype(b16)
-
+        block = midall[:, :, s].astype(f32).reshape(128, FT).astype(b16)
+        vuv[:, s] = jnp.dot(gvp_t[...], block, preferred_element_type=f32).astype(b16)
+
+    vu_out = pltpu.make_async_copy(vuv, gvu_h, lsem.at[5])
+    vu_out.start()
     gn = s2.finish() * mgain[...]
     uhat = mid[...] * recip
     back = recip * (gn - uhat * jnp.mean(gn * uhat, axis=-1, keepdims=True))
     gvin[...] = (nat[pl.ds(pl.multiple_of(d * 8, 8), 8), :] + back).astype(b16)
     for one in sent:
         one.wait_send()
-
-
-def weights_kernel(normed, gp, hid_t, br, gvp_t, midn, gvin, gpw, gvd, gvu, out):
-    f32, b16 = jnp.float32, jnp.bfloat16
-    step = pl.program_id(0)
-    gpw[...] = contract_rows(normed[...], gp[...]).astype(b16)
-
-    @pl.when(step % 5 == 0)
-    def _():
-        gvd[...] = jnp.dot(hid_t[...], br[...], preferred_element_type=f32).astype(b16)
-
-    @pl.when(step % 5 == 2)
-    def _():
-        gvu[...] = jnp.dot(gvp_t[...], midn[...], preferred_element_type=f32).astype(b16)
-
-    @pl.when(step == 0)
+    vd_out.wait()
+    vu_out.wait()
+
+
+def weights_kernel(normed, gp, gvd_in, gvu_in, gvin, gpw, gvd, gvu, out):
+    gpw[...] = contract_rows(normed[...], gp[...]).astype(jnp.bfloat16)
+    gvd[...] = gvd_in[...]
+    gvu[...] = gvu_in[...]
+
+    @pl.when(pl.program_id(0) == 0)
     def _():
         out[...] = gvin[...]
 
@@ -521,14 +530,14 @@
         ((32, features), f32), ((128, d_vit), f32), ((32, width), f32),
         ((units, 128), f32), ((units, 128), f32), ((8, d_vit), f32), ((1, features), f32),
         ((1, features), f32), ((1, d_vit), f32), ((1, d_vit), f32), ((32, 128), f32),
-        ((4, 8, 128), f32),
+        ((4, 8, 128), f32), ((units, 128), b16), ((128, d_vit), b16), ((units, 128), b16),
     ]
-    outs = [(32, features), (32, width), (units, 128), (128, d_vit), (units, 128), (128, d_vit), (8, d_vit)]
+    outs = [(32, features), (32, width), (units, d_vit), (units, d_vit), (8, d_vit)]
     held = pl.pallas_call(
         fused_kernel,
         out_shape=[jax.ShapeDtypeStruct(shape, b16) for shape in outs],
         in_specs=[vmem] * 14 + [hbm] * 3,
-        out_specs=[vmem] * len(outs),
+        out_specs=[vmem, vmem, hbm, hbm, vmem],
         scratch_shapes=[pltpu.VMEM(s, t) for s, t in scratch]
         + [
             pltpu.SemaphoreType.DMA((6,)), pltpu.SemaphoreType.DMA((80,)),
@@ -550,23 +559,21 @@
     )
     steps = 25
     whole = lambda i: (0, 0)
-    fifth = lambda i: (0, i // 5)
+    vit_rows = pl.BlockSpec((units // steps, d_vit), lambda i: (i, 0))
     gpw, gvd, gvu, gvin = pl.pallas_call(
         weights_kernel,
         grid=(steps,),
         in_specs=[
             pl.BlockSpec((32, features // steps), lambda i: (0, i)),
             pl.BlockSpec((32, width), whole),
-            pl.BlockSpec((units, 128), whole),
-            pl.BlockSpec((128, FT), fifth),
-            pl.BlockSpec((units, 128), whole),
-            pl.BlockSpec((128, FT), fifth),
+            vit_rows,
+            vit_rows,
             pl.BlockSpec((8, d_vit), whole),
         ],
         out_specs=[
             pl.BlockSpec((features // steps, width), lambda i: (i, 0)),
-            pl.BlockSpec((units, FT), fifth),
-            pl.BlockSpec((units, FT), fifth),
+            vit_rows,
+            vit_rows,
             pl.BlockSpec((8, d_vit), whole),
         ],
         out_shape=[
@@ -575,7 +582,7 @@
             jax.ShapeDtypeStruct((units, d_vit), b16),
             jax.ShapeDtypeStruct((8, d_vit), b16),
         ],
-        compiler_params=pltpu.CompilerParams(vmem_limit_bytes=24 * 2**20),
+        compiler_params=pltpu.CompilerParams(vmem_limit_bytes=60 * 2**20),
     )(*held)
     return gpw, gvd, gvu.T, gvin
 

time: 97.5 us -> 94.7 us (0.971)
  local copies, waits for them, and re-layouts: 8.21 us -> 1.37 us
  Pallas kernels: 88.2 us -> 91.9 us
    unnamed x15 -> x1, local copies, waits for them, and re-layouts: 8.21 us -> 1.37 us
    pallas_call x1, Pallas kernels: 19.9 us -> 25.9 us  [fused_body(): pl.pallas_call(weights_kernel, grid=(steps,), in_specs=[pl.BlockSpec((32,...]
    pallas_call x1, Pallas kernels: 68.2 us -> 66.1 us  [fused_body(): pl.pallas_call(fused_kernel, out_shape=[jax.ShapeDtypeStruct(shape, b16)...]
where the time goes in v3:
time: 94.7 us; the launch traced here: 94 us
  Pallas kernels  91.9 us (97%)
  local copies, waits for them, and re-layouts  1.37 us (1%)
    pallas_call x1, Pallas kernels, fused_body(): pl.pallas_call(fused_kernel, out_shape=[jax.ShapeDtypeStruct(shape, b16)...  66.1 us
    pallas_call x1, Pallas kernels, fused_body(): pl.pallas_call(weights_kernel, grid=(steps,), in_specs=[pl.BlockSpec((32,...  25.9 us

profile of v3, /device:TPU:0, one launch (start us, length us, event | category | flops | bytes accessed | tf_op | source)
XLA Modules:
  0.0 94.0 jit_solution(15045786415593551942)
XLA Ops:
  0.6 1.4 %copy.21.ppe = s32[32,4]{1,0:T(8,128)} copy(s32[32,4]{0,1:T(4,128)} %param.20) | data formatting | bytes 1024 | tf_op args[3]
  2.0 66.1 %shard_map.192 = (bf16[32,12800]{1,0:T(8,128)(2,1)}, bf16[32,512]{1,0:T(8,128)(2,1)}, bf16[800,3200]{1,0:T(8,128)(2,1)}, bf16[800,3200]{1,0:T(8,128)(2,1)}, bf16[8,3200]{1,0:T(8,128)(2,1)}) custom-call(bf16[2,8192]{1,0:T(2,128)(2,1)} %gdec.1, s32[1,32]{1,0:T(1,128)} %bitcast.14, bf16[32,512]{1,0:T(8,128)(2,1)} %ppc.1, s32[32,4]{1,0:T(8,128)} %copy.21.ppe, ...), custom_call_target="tpu_custom_call" | custom-call | flops 2000000000 | bytes 24000000 | tf_op jit(solution)/shard_map/pallas_call | solution.py:536
  68.1 25.9 %shard_map.193 = (bf16[12800,512]{1,0:T(8,128)(2,1)}, bf16[800,3200]{1,0:T(8,128)(2,1)}, bf16[800,3200]{1,0:T(8,128)(2,1)}, bf16[8,3200]{1,0:T(8,128)(2,1)}) custom-call(bf16[32,12800]{1,0:T(8,128)(2,1)} %get-tuple-element.13.normed, bf16[32,512]{1,0:T(8,128)(2,1)} %get-tuple-element.14.gp, bf16[800,3200]{1,0:T(8,128)(2,1)} %get-tuple-element.15.gvd_in, ...), custom_call_target="tpu_custom_call" | custom-call | tf_op jit(solution)/shard_map/pallas_call | solution.py:563
